TPU v7x, 256 devices: a whole 4x4x8 slice. The times are simulated.
256 devices in a mesh: seq: 32 (over x, z_lo, core), head: 8 (over y, z_hi).
Axes of the slice: x: 4, y: 4, z: 8 (z_hi: 2, z_lo: 4; z = z_hi * 4 + z_lo), core: 2. Of those that a mesh axis runs over, the one named last changes fastest.
Arguments:
- query_states: bfloat16 [8192, 8192], P(('seq', 'head')), may hold values from -8 to 8
- key_states: bfloat16 [8192, 1024], P(('seq', 'head')), may hold values from -8 to 8
- value_states: bfloat16 [8192, 1024], P(('seq', 'head')), may hold values from -6 to 6
- seg_ids: int32 [8192], P('seq'), may hold values from 0 to 9, as said below
- seg_starts: int32 [10], replicated, may hold values from 0 to 7168, as said below
Outputs:
- attended: bfloat16 [8192, 8192], P(('seq', 'head'))
Inputs may be any that keep to these rules, and one draw needn't show every extreme that they name: `seg_ids`: 0 on a prompt at the start, 1 to 8 on the eight responses in order, 9 on a summary at the end; never falling; the prompt holds 512 to 1024 positions, the summary exactly 1024. `seg_starts`: entry 0 is 0, entries rise strictly, entry 9 is 7168.
All inputs are finite; a program needn't handle non-finite values.
Results may differ from a plain program's by a relative error of at most 0.0045.
Values may be sent and summed in bfloat16 or wider, within the bound.
A program may use at most 64 MiB of HBM per device.

v0:
```python
import math

import jax
import jax.numpy as jnp
from jax import lax
from jax.sharding import PartitionSpec as P

HD = 128


NEG_FILL = -1e30


def visible_keys(query_pos, query_seg, own_start, key_pos, first_response):
    causal = key_pos[None, :] <= query_pos[:, None]
    allowed = (
        (key_pos[None, :] < first_response)
        | (key_pos[None, :] >= own_start[:, None])
        | (query_seg[:, None] == 9)
    )
    return causal & allowed


def segment_start(seg_rows, seg_starts):
    labels = jnp.arange(10, dtype=jnp.int32)
    picked = jnp.where(seg_rows[:, None] == labels[None, :], seg_starts[None, :], 0)
    return jnp.sum(picked, axis=1)


def per_device(query_states, key_states, value_states, seg_ids, seg_starts):
    query_local, key_local, value_local = (
        lax.all_to_all(query_states, "head", split_axis=1, concat_axis=0, tiled=True),
        lax.all_to_all(key_states, "head", split_axis=1, concat_axis=0, tiled=True),
        lax.all_to_all(value_states, "head", split_axis=1, concat_axis=0, tiled=True),
    )
    block_rows = query_local.shape[0]
    query_width = query_local.shape[1]
    kv_local = key_local.shape[1] // HD
    group_size = query_width // (kv_local * HD)
    seq_index = lax.axis_index("seq")
    own_pos = seq_index * block_rows + jnp.arange(block_rows, dtype=jnp.int32)
    score_scale = 1.0 / math.sqrt(HD)
    own_start = segment_start(seg_ids, seg_starts)
    first_response = seg_starts[1]
    query_heads = query_local.reshape(block_rows, kv_local, group_size, HD)
    all_keys, all_values = (
        lax.all_gather(key_local, "seq", axis=0, tiled=True),
        lax.all_gather(value_local, "seq", axis=0, tiled=True),
    )
    context_rows = all_keys.shape[0]
    step_rows = math.gcd(1024, context_rows)

    def one_tile(tile_index, state):
        tile_start = tile_index * step_rows
        key_tile = lax.dynamic_slice_in_dim(all_keys, tile_start, step_rows, 0).reshape(
            step_rows, kv_local, HD
        )
        value_tile = lax.dynamic_slice_in_dim(all_values, tile_start, step_rows, 0).reshape(
            step_rows, kv_local, HD
        )
        key_pos = tile_start + jnp.arange(step_rows, dtype=jnp.int32)
        visible = visible_keys(own_pos, seg_ids, own_start, key_pos, first_response)
        running_max, running_sum, running_acc = state
        scores = (
            jnp.einsum("rhgd,khd->rhgk", query_heads, key_tile, preferred_element_type=jnp.float32)
            * score_scale
        )
        mask_wide = visible[:, None, None, :]
        scores = jnp.where(mask_wide, scores, NEG_FILL)
        new_max = jnp.maximum(running_max, jnp.max(scores, axis=3))
        weights = jnp.where(mask_wide, jnp.exp(scores - new_max[..., None]), 0.0)
        factor = jnp.exp(running_max - new_max)
        new_sum = running_sum * factor + jnp.sum(weights, axis=3)
        mixed_tile = jnp.einsum(
            "rhgk,khd->rhgd",
            weights.astype(jnp.bfloat16),
            value_tile,
            preferred_element_type=jnp.float32,
        )
        return (new_max, new_sum, running_acc * factor[..., None] + mixed_tile)

    init_state = (
        jnp.full((block_rows, kv_local, group_size), NEG_FILL, jnp.float32),
        jnp.zeros((block_rows, kv_local, group_size), jnp.float32),
        jnp.zeros((block_rows, kv_local, group_size, HD), jnp.float32),
    )
    final_max, final_sum, final_acc = lax.fori_loop(
        0, context_rows // step_rows, one_tile, init_state
    )
    attended_rows = (
        (final_acc / final_sum[..., None]).reshape(block_rows, query_width).astype(jnp.bfloat16)
    )
    return lax.all_to_all(attended_rows, "head", split_axis=0, concat_axis=1, tiled=True)


def solution(mesh):
    return jax.shard_map(
        per_device,
        mesh=mesh,
        in_specs=(
            P(("seq", "head"), None),
            P(("seq", "head"), None),
            P(("seq", "head"), None),
            P("seq"),
            P(),
        ),
        out_specs=P(("seq", "head"), None),
        check_vma=False,
    )
```

profile of v0, /device:TPU:3, one launch (start us, length us, event | category | flops | bytes accessed | tf_op | source)
XLA Modules:
  0.0 314.5 jit_solution(545245052855133164)
XLA Ops:
  7.4 19.8 %all_to_all.70 = bf16[32,8,128]{2,0,1:T(8,128)(2,1)} all-to-all(bf16[32,8,128]{2,0,1:T(8,128)(2,1)S(1)} %copy_bitcast_fusion.2), channel_id=1, replica_groups=mesh['seq'=32,'head'=8] {'head'}, dimensions={1} | all-to-all | bytes 131072 | tf_op jit(solution)/shard_map/all_to_all | solution.py:33
  28.1 12.2 %all_to_all.71 = bf16[32,8,128]{2,0,1:T(8,128)(2,1)} all-to-all(bf16[32,8,128]{2,0,1:T(8,128)(2,1)S(1)} %copy_bitcast_fusion.1), channel_id=1, replica_groups=mesh['seq'=32,'head'=8] {'head'}, dimensions={1} | all-to-all | bytes 131072 | tf_op jit(solution)/shard_map/all_to_all | solution.py:34
  42.2 3.5 %all-to-all-start.1 = ((bf16[32,8,1024]{2,0,1:T(8,128)(2,1)}), bf16[32,8,1024]{2,0,1:T(8,128)(2,1)S(1)}, u32[]{:S(2)}, u32[]{:S(2)}) async-start(bf16[32,8,1024]{2,0,1:T(8,128)(2,1)} %bitcast.88), calls=%async_computation.1 | async-start | bytes 1048576 | tf_op jit(solution)/shard_map/all_to_all | solution.py:32
  47.8 9.5 %all-to-all-done.1 = bf16[32,8,1024]{2,0,1:T(8,128)(2,1)S(1)} async-done(((bf16[32,8,1024]{2,0,1:T(8,128)(2,1)}), bf16[32,8,1024]{2,0,1:T(8,128)(2,1)S(1)}, u32[]{:S(2)}, u32[]{:S(2)}) %all-to-all-start.1) | async-done | bytes 524320 | tf_op jit(solution)/shard_map/all_to_all | solution.py:32
  57.5 31.8 %all-gather.3.cloned.1.call-done = bf16[8192,128]{1,0:T(8,128)(2,1)} async-done(((bf16[256,128]{1,0:T(8,128)(2,1)}), bf16[8192,128]{1,0:T(8,128)(2,1)}) %all-gather.3.cloned.1.call-update) | async-done | bytes 2097168 | tf_op jit(solution)/shard_map/all_gather | solution.py:47
  89.3 67.2 %all-gather.5.cloned.1.call-done = bf16[8192,128]{1,0:T(8,128)(2,1)} async-done(((bf16[256,128]{1,0:T(8,128)(2,1)}), bf16[8192,128]{1,0:T(8,128)(2,1)}) %all-gather.5.cloned.1.call-update) | async-done | bytes 2097168 | tf_op jit(solution)/shard_map/all_gather | solution.py:48
  156.5 127.8 %while.18 = (s32[]{:T(128)}, f32[256,1,8]{0,2,1:T(8,128)S(1)}, f32[256,1,8]{0,2,1:T(8,128)S(1)}, f32[256,1,8,128]{0,3,2,1:T(8,128)S(1)}, s32[]{:T(128)}, /*index...) while((s32[]{:T(128)}, f32[256,1,8]{0,2,1:T(8,128)S(1)}, ...), condition=%wide.region_4.5_spmd.clone, body=%wide.region_1.4_spmd.clone.sunk | while | flops 1103117824 | bytes 54672140 | solution.py:87
  158.7 5.6 %fusion.37 = (f32[256,8]{0,1:T(8,128)S(1)}, f32[1024,256,8]{1,0,2:T(8,128)}) fusion(pred[256,1024]{0,1:T(8,128)(4,1)S(1)} %or_and_fusion.2, bf16[256,1,8,128]{3,0,2,1:T(8,128)(2,1)S(1)} %get-tuple-element.414, bf16[8192,128]{1,0:T(8,128)(2,1)} %get-tuple-element.413, s32[]{:T(128)S(6)} %select_n.71), kind=kOutput, calls=%fused_computation.3.clone.1 | convolution fusion | flops 543160320 | bytes 9445380 | tf_op jit(solution)/shard_map/while/body/eval_jaxpr/rhgd,khd->rhgk/dot_general | solution.py:65
  164.3 6.1 %fusion.40 = f32[256,1,8,128]{0,3,2,1:T(8,128)S(1)} fusion(f32[1024,256,8]{1,0,2:T(8,128)} %get-tuple-element.374, f32[256,8]{0,1:T(8,128)S(1)} %bitcast.113, pred[256,1024]{0,1:T(8,128)(4,1)S(1)} %or_and_fusion.2, f32[256,1,8,128]{0,3,2,1:T(8,128)S(1)} %get-tuple-element.394, f32[256,8]{0,1:T(8,128)S(1)} %get-tuple-element.375, pred[]{:T(512)S(6)} %compare.3, ...), kind=kOutput, calls=%fused_computation.10.clone.1 | convolution fusion | flops 548143104 | bytes 11026437 | tf_op jit(solution)/shard_map/while/body/eval_jaxpr/rhgk,khd->rhgd/dot_general | solution.py:74
  174.6 5.6 %fusion.37 = (f32[256,8]{0,1:T(8,128)S(1)}, f32[1024,256,8]{1,0,2:T(8,128)}) fusion(pred[256,1024]{0,1:T(8,128)(4,1)S(1)} %or_and_fusion.2, bf16[256,1,8,128]{3,0,2,1:T(8,128)(2,1)S(1)} %get-tuple-element.414, bf16[8192,128]{1,0:T(8,128)(2,1)} %get-tuple-element.413, s32[]{:T(128)S(6)} %select_n.71), kind=kOutput, calls=%fused_computation.3.clone.1 | convolution fusion | flops 543160320 | bytes 9445380 | tf_op jit(solution)/shard_map/while/body/eval_jaxpr/rhgd,khd->rhgk/dot_general | solution.py:65
  180.3 6.1 %fusion.40 = f32[256,1,8,128]{0,3,2,1:T(8,128)S(1)} fusion(f32[1024,256,8]{1,0,2:T(8,128)} %get-tuple-element.374, f32[256,8]{0,1:T(8,128)S(1)} %bitcast.113, pred[256,1024]{0,1:T(8,128)(4,1)S(1)} %or_and_fusion.2, f32[256,1,8,128]{0,3,2,1:T(8,128)S(1)} %get-tuple-element.394, f32[256,8]{0,1:T(8,128)S(1)} %get-tuple-element.375, pred[]{:T(512)S(6)} %compare.3, ...), kind=kOutput, calls=%fused_computation.10.clone.1 | convolution fusion | flops 548143104 | bytes 11026437 | tf_op jit(solution)/shard_map/while/body/eval_jaxpr/rhgk,khd->rhgd/dot_general | solution.py:74
  190.6 5.6 %fusion.37 = (f32[256,8]{0,1:T(8,128)S(1)}, f32[1024,256,8]{1,0,2:T(8,128)}) fusion(pred[256,1024]{0,1:T(8,128)(4,1)S(1)} %or_and_fusion.2, bf16[256,1,8,128]{3,0,2,1:T(8,128)(2,1)S(1)} %get-tuple-element.414, bf16[8192,128]{1,0:T(8,128)(2,1)} %get-tuple-element.413, s32[]{:T(128)S(6)} %select_n.71), kind=kOutput, calls=%fused_computation.3.clone.1 | convolution fusion | flops 543160320 | bytes 9445380 | tf_op jit(solution)/shard_map/while/body/eval_jaxpr/rhgd,khd->rhgk/dot_general | solution.py:65
  196.2 6.1 %fusion.40 = f32[256,1,8,128]{0,3,2,1:T(8,128)S(1)} fusion(f32[1024,256,8]{1,0,2:T(8,128)} %get-tuple-element.374, f32[256,8]{0,1:T(8,128)S(1)} %bitcast.113, pred[256,1024]{0,1:T(8,128)(4,1)S(1)} %or_and_fusion.2, f32[256,1,8,128]{0,3,2,1:T(8,128)S(1)} %get-tuple-element.394, f32[256,8]{0,1:T(8,128)S(1)} %get-tuple-element.375, pred[]{:T(512)S(6)} %compare.3, ...), kind=kOutput, calls=%fused_computation.10.clone.1 | convolution fusion | flops 548143104 | bytes 11026437 | tf_op jit(solution)/shard_map/while/body/eval_jaxpr/rhgk,khd->rhgd/dot_general | solution.py:74
  206.6 5.6 %fusion.37 = (f32[256,8]{0,1:T(8,128)S(1)}, f32[1024,256,8]{1,0,2:T(8,128)}) fusion(pred[256,1024]{0,1:T(8,128)(4,1)S(1)} %or_and_fusion.2, bf16[256,1,8,128]{3,0,2,1:T(8,128)(2,1)S(1)} %get-tuple-element.414, bf16[8192,128]{1,0:T(8,128)(2,1)} %get-tuple-element.413, s32[]{:T(128)S(6)} %select_n.71), kind=kOutput, calls=%fused_computation.3.clone.1 | convolution fusion | flops 543160320 | bytes 9445380 | tf_op jit(solution)/shard_map/while/body/eval_jaxpr/rhgd,khd->rhgk/dot_general | solution.py:65
  212.2 6.1 %fusion.40 = f32[256,1,8,128]{0,3,2,1:T(8,128)S(1)} fusion(f32[1024,256,8]{1,0,2:T(8,128)} %get-tuple-element.374, f32[256,8]{0,1:T(8,128)S(1)} %bitcast.113, pred[256,1024]{0,1:T(8,128)(4,1)S(1)} %or_and_fusion.2, f32[256,1,8,128]{0,3,2,1:T(8,128)S(1)} %get-tuple-element.394, f32[256,8]{0,1:T(8,128)S(1)} %get-tuple-element.375, pred[]{:T(512)S(6)} %compare.3, ...), kind=kOutput, calls=%fused_computation.10.clone.1 | convolution fusion | flops 548143104 | bytes 11026437 | tf_op jit(solution)/shard_map/while/body/eval_jaxpr/rhgk,khd->rhgd/dot_general | solution.py:74
  222.6 5.6 %fusion.37 = (f32[256,8]{0,1:T(8,128)S(1)}, f32[1024,256,8]{1,0,2:T(8,128)}) fusion(pred[256,1024]{0,1:T(8,128)(4,1)S(1)} %or_and_fusion.2, bf16[256,1,8,128]{3,0,2,1:T(8,128)(2,1)S(1)} %get-tuple-element.414, bf16[8192,128]{1,0:T(8,128)(2,1)} %get-tuple-element.413, s32[]{:T(128)S(6)} %select_n.71), kind=kOutput, calls=%fused_computation.3.clone.1 | convolution fusion | flops 543160320 | bytes 9445380 | tf_op jit(solution)/shard_map/while/body/eval_jaxpr/rhgd,khd->rhgk/dot_general | solution.py:65
  228.2 6.1 %fusion.40 = f32[256,1,8,128]{0,3,2,1:T(8,128)S(1)} fusion(f32[1024,256,8]{1,0,2:T(8,128)} %get-tuple-element.374, f32[256,8]{0,1:T(8,128)S(1)} %bitcast.113, pred[256,1024]{0,1:T(8,128)(4,1)S(1)} %or_and_fusion.2, f32[256,1,8,128]{0,3,2,1:T(8,128)S(1)} %get-tuple-element.394, f32[256,8]{0,1:T(8,128)S(1)} %get-tuple-element.375, pred[]{:T(512)S(6)} %compare.3, ...), kind=kOutput, calls=%fused_computation.10.clone.1 | convolution fusion | flops 548143104 | bytes 11026437 | tf_op jit(solution)/shard_map/while/body/eval_jaxpr/rhgk,khd->rhgd/dot_general | solution.py:74
  238.5 5.6 %fusion.37 = (f32[256,8]{0,1:T(8,128)S(1)}, f32[1024,256,8]{1,0,2:T(8,128)}) fusion(pred[256,1024]{0,1:T(8,128)(4,1)S(1)} %or_and_fusion.2, bf16[256,1,8,128]{3,0,2,1:T(8,128)(2,1)S(1)} %get-tuple-element.414, bf16[8192,128]{1,0:T(8,128)(2,1)} %get-tuple-element.413, s32[]{:T(128)S(6)} %select_n.71), kind=kOutput, calls=%fused_computation.3.clone.1 | convolution fusion | flops 543160320 | bytes 9445380 | tf_op jit(solution)/shard_map/while/body/eval_jaxpr/rhgd,khd->rhgk/dot_general | solution.py:65
  244.2 6.1 %fusion.40 = f32[256,1,8,128]{0,3,2,1:T(8,128)S(1)} fusion(f32[1024,256,8]{1,0,2:T(8,128)} %get-tuple-element.374, f32[256,8]{0,1:T(8,128)S(1)} %bitcast.113, pred[256,1024]{0,1:T(8,128)(4,1)S(1)} %or_and_fusion.2, f32[256,1,8,128]{0,3,2,1:T(8,128)S(1)} %get-tuple-element.394, f32[256,8]{0,1:T(8,128)S(1)} %get-tuple-element.375, pred[]{:T(512)S(6)} %compare.3, ...), kind=kOutput, calls=%fused_computation.10.clone.1 | convolution fusion | flops 548143104 | bytes 11026437 | tf_op jit(solution)/shard_map/while/body/eval_jaxpr/rhgk,khd->rhgd/dot_general | solution.py:74
  254.5 5.6 %fusion.37 = (f32[256,8]{0,1:T(8,128)S(1)}, f32[1024,256,8]{1,0,2:T(8,128)}) fusion(pred[256,1024]{0,1:T(8,128)(4,1)S(1)} %or_and_fusion.2, bf16[256,1,8,128]{3,0,2,1:T(8,128)(2,1)S(1)} %get-tuple-element.414, bf16[8192,128]{1,0:T(8,128)(2,1)} %get-tuple-element.413, s32[]{:T(128)S(6)} %select_n.71), kind=kOutput, calls=%fused_computation.3.clone.1 | convolution fusion | flops 543160320 | bytes 9445380 | tf_op jit(solution)/shard_map/while/body/eval_jaxpr/rhgd,khd->rhgk/dot_general | solution.py:65
  260.1 6.1 %fusion.40 = f32[256,1,8,128]{0,3,2,1:T(8,128)S(1)} fusion(f32[1024,256,8]{1,0,2:T(8,128)} %get-tuple-element.374, f32[256,8]{0,1:T(8,128)S(1)} %bitcast.113, pred[256,1024]{0,1:T(8,128)(4,1)S(1)} %or_and_fusion.2, f32[256,1,8,128]{0,3,2,1:T(8,128)S(1)} %get-tuple-element.394, f32[256,8]{0,1:T(8,128)S(1)} %get-tuple-element.375, pred[]{:T(512)S(6)} %compare.3, ...), kind=kOutput, calls=%fused_computation.10.clone.1 | convolution fusion | flops 548143104 | bytes 11026437 | tf_op jit(solution)/shard_map/while/body/eval_jaxpr/rhgk,khd->rhgd/dot_general | solution.py:74
  270.5 5.6 %fusion.37 = (f32[256,8]{0,1:T(8,128)S(1)}, f32[1024,256,8]{1,0,2:T(8,128)}) fusion(pred[256,1024]{0,1:T(8,128)(4,1)S(1)} %or_and_fusion.2, bf16[256,1,8,128]{3,0,2,1:T(8,128)(2,1)S(1)} %get-tuple-element.414, bf16[8192,128]{1,0:T(8,128)(2,1)} %get-tuple-element.413, s32[]{:T(128)S(6)} %select_n.71), kind=kOutput, calls=%fused_computation.3.clone.1 | convolution fusion | flops 543160320 | bytes 9445380 | tf_op jit(solution)/shard_map/while/body/eval_jaxpr/rhgd,khd->rhgk/dot_general | solution.py:65
  276.1 6.1 %fusion.40 = f32[256,1,8,128]{0,3,2,1:T(8,128)S(1)} fusion(f32[1024,256,8]{1,0,2:T(8,128)} %get-tuple-element.374, f32[256,8]{0,1:T(8,128)S(1)} %bitcast.113, pred[256,1024]{0,1:T(8,128)(4,1)S(1)} %or_and_fusion.2, f32[256,1,8,128]{0,3,2,1:T(8,128)S(1)} %get-tuple-element.394, f32[256,8]{0,1:T(8,128)S(1)} %get-tuple-element.375, pred[]{:T(512)S(6)} %compare.3, ...), kind=kOutput, calls=%fused_computation.10.clone.1 | convolution fusion | flops 548143104 | bytes 11026437 | tf_op jit(solution)/shard_map/while/body/eval_jaxpr/rhgk,khd->rhgd/dot_general | solution.py:74
  285.0 21.8 %all_to_all.72 = bf16[8,32,1024]{2,1,0:T(8,128)(2,1)S(1)} all-to-all(bf16[8,32,1024]{2,1,0:T(8,128)(2,1)S(1)} %convert_element_type.15), channel_id=1, replica_groups=mesh['seq'=32,'head'=8] {'head'}, dimensions={0} | all-to-all | bytes 1048576 | tf_op jit(solution)/shard_map/all_to_all | solution.py:93
  (132 shorter events, 41.0 us)
Async XLA Ops:
  6.5 0.8 copy-start
  6.5 82.7 %all-gather.3.cloned.1.call-start = ((), (), s32[]{:S(2)}) async-start(), calls=%async_computation.4 | async-start | bytes 2162688 | tf_op jit(solution)/shard_map/all_gather | solution.py:47
  27.2 129.3 %all-gather.5.cloned.1.call-start = ((), (), s32[]{:S(2)}) async-start(), calls=%async_computation.5 | async-start | bytes 2162688 | tf_op jit(solution)/shard_map/all_gather | solution.py:48
  42.2 15.1 %all-to-all-start.1 = ((bf16[32,8,1024]{2,0,1:T(8,128)(2,1)}), bf16[32,8,1024]{2,0,1:T(8,128)(2,1)S(1)}, u32[]{:S(2)}, u32[]{:S(2)}) async-start(bf16[32,8,1024]{2,0,1:T(8,128)(2,1)} %bitcast.88), calls=%async_computation.1 | async-start | bytes 1048576 | tf_op jit(solution)/shard_map/all_to_all | solution.py:32
  164.3 6.1 %slice-start = ((s8[8388608]{0:T(1024)(128)(4,1)}), s8[4194304]{0:T(1024)(128)(4,1)S(1)}, s32[]{:S(2)}) async-start(s8[8388608]{0:T(1024)(128)(4,1)} %bitcast.111), calls=%async_computation.6 | async-start | bytes 8388608 | tf_op jit(solution)/shard_map/while
  164.3 6.1 %slice-start.1 = ((s8[8388608]{0:T(1024)(128)(4,1)}), s8[4194304]{0:T(1024)(128)(4,1)S(1)}, s32[]{:S(2)}) async-start(s8[8388608]{0:T(1024)(128)(4,1)} %bitcast.111), calls=%async_computation.7 | async-start | bytes 8388608 | tf_op jit(solution)/shard_map/while
  180.2 6.1 %slice-start = ((s8[8388608]{0:T(1024)(128)(4,1)}), s8[4194304]{0:T(1024)(128)(4,1)S(1)}, s32[]{:S(2)}) async-start(s8[8388608]{0:T(1024)(128)(4,1)} %bitcast.111), calls=%async_computation.6 | async-start | bytes 8388608 | tf_op jit(solution)/shard_map/while
  180.3 6.1 %slice-start.1 = ((s8[8388608]{0:T(1024)(128)(4,1)}), s8[4194304]{0:T(1024)(128)(4,1)S(1)}, s32[]{:S(2)}) async-start(s8[8388608]{0:T(1024)(128)(4,1)} %bitcast.111), calls=%async_computation.7 | async-start | bytes 8388608 | tf_op jit(solution)/shard_map/while
  196.2 6.1 %slice-start = ((s8[8388608]{0:T(1024)(128)(4,1)}), s8[4194304]{0:T(1024)(128)(4,1)S(1)}, s32[]{:S(2)}) async-start(s8[8388608]{0:T(1024)(128)(4,1)} %bitcast.111), calls=%async_computation.6 | async-start | bytes 8388608 | tf_op jit(solution)/shard_map/while
  196.2 6.1 %slice-start.1 = ((s8[8388608]{0:T(1024)(128)(4,1)}), s8[4194304]{0:T(1024)(128)(4,1)S(1)}, s32[]{:S(2)}) async-start(s8[8388608]{0:T(1024)(128)(4,1)} %bitcast.111), calls=%async_computation.7 | async-start | bytes 8388608 | tf_op jit(solution)/shard_map/while
  212.2 6.1 %slice-start = ((s8[8388608]{0:T(1024)(128)(4,1)}), s8[4194304]{0:T(1024)(128)(4,1)S(1)}, s32[]{:S(2)}) async-start(s8[8388608]{0:T(1024)(128)(4,1)} %bitcast.111), calls=%async_computation.6 | async-start | bytes 8388608 | tf_op jit(solution)/shard_map/while
  212.2 6.1 %slice-start.1 = ((s8[8388608]{0:T(1024)(128)(4,1)}), s8[4194304]{0:T(1024)(128)(4,1)S(1)}, s32[]{:S(2)}) async-start(s8[8388608]{0:T(1024)(128)(4,1)} %bitcast.111), calls=%async_computation.7 | async-start | bytes 8388608 | tf_op jit(solution)/shard_map/while
  228.2 6.1 %slice-start = ((s8[8388608]{0:T(1024)(128)(4,1)}), s8[4194304]{0:T(1024)(128)(4,1)S(1)}, s32[]{:S(2)}) async-start(s8[8388608]{0:T(1024)(128)(4,1)} %bitcast.111), calls=%async_computation.6 | async-start | bytes 8388608 | tf_op jit(solution)/shard_map/while
  228.2 6.1 %slice-start.1 = ((s8[8388608]{0:T(1024)(128)(4,1)}), s8[4194304]{0:T(1024)(128)(4,1)S(1)}, s32[]{:S(2)}) async-start(s8[8388608]{0:T(1024)(128)(4,1)} %bitcast.111), calls=%async_computation.7 | async-start | bytes 8388608 | tf_op jit(solution)/shard_map/while
  244.1 6.1 %slice-start = ((s8[8388608]{0:T(1024)(128)(4,1)}), s8[4194304]{0:T(1024)(128)(4,1)S(1)}, s32[]{:S(2)}) async-start(s8[8388608]{0:T(1024)(128)(4,1)} %bitcast.111), calls=%async_computation.6 | async-start | bytes 8388608 | tf_op jit(solution)/shard_map/while
  244.2 6.1 %slice-start.1 = ((s8[8388608]{0:T(1024)(128)(4,1)}), s8[4194304]{0:T(1024)(128)(4,1)S(1)}, s32[]{:S(2)}) async-start(s8[8388608]{0:T(1024)(128)(4,1)} %bitcast.111), calls=%async_computation.7 | async-start | bytes 8388608 | tf_op jit(solution)/shard_map/while
  260.1 6.1 %slice-start = ((s8[8388608]{0:T(1024)(128)(4,1)}), s8[4194304]{0:T(1024)(128)(4,1)S(1)}, s32[]{:S(2)}) async-start(s8[8388608]{0:T(1024)(128)(4,1)} %bitcast.111), calls=%async_computation.6 | async-start | bytes 8388608 | tf_op jit(solution)/shard_map/while
  260.1 6.1 %slice-start.1 = ((s8[8388608]{0:T(1024)(128)(4,1)}), s8[4194304]{0:T(1024)(128)(4,1)S(1)}, s32[]{:S(2)}) async-start(s8[8388608]{0:T(1024)(128)(4,1)} %bitcast.111), calls=%async_computation.7 | async-start | bytes 8388608 | tf_op jit(solution)/shard_map/while
  276.1 6.1 %slice-start = ((s8[8388608]{0:T(1024)(128)(4,1)}), s8[4194304]{0:T(1024)(128)(4,1)S(1)}, s32[]{:S(2)}) async-start(s8[8388608]{0:T(1024)(128)(4,1)} %bitcast.111), calls=%async_computation.6 | async-start | bytes 8388608 | tf_op jit(solution)/shard_map/while
  276.1 6.1 %slice-start.1 = ((s8[8388608]{0:T(1024)(128)(4,1)}), s8[4194304]{0:T(1024)(128)(4,1)S(1)}, s32[]{:S(2)}) async-start(s8[8388608]{0:T(1024)(128)(4,1)} %bitcast.111), calls=%async_computation.7 | async-start | bytes 8388608 | tf_op jit(solution)/shard_map/while
Sparse Core Ops, SparseCore 0:
  27.4 61.8 all-gather.2
  91.1 65.3 all-gather.4
where the time goes:
time: 320 us; the launch traced here: 314 us
  waiting for transfers between devices  109 us (34%)
  matrix products  93.3 us (29%)
  blocking collectives  53.8 us (17%)
  other arithmetic  34.4 us (11%)
  between operations  13.5 us (4%)
  local copies, waits for them, and re-layouts  6.47 us (2%)
  starting transfers between devices  3.54 us (1%)
    all_gather x1, waiting for transfers between devices, per_device(): lax.all_gather(value_local, 'seq', axis=0, tiled=True)  67.2 us
    dot_general x8, matrix products, one_tile(): jnp.einsum('rhgk,khd->rhgd', weights.astype(jnp.bfloat16), value_tile, pr...  48.4 us
    dot_general x8, matrix products, one_tile(): jnp.einsum('rhgd,khd->rhgk', query_heads, key_tile, preferred_element_typ...  44.9 us
    all_gather x1, waiting for transfers between devices, per_device(): lax.all_gather(key_local, 'seq', axis=0, tiled=True)  31.8 us
    all_to_all x1, blocking collectives, per_device(): lax.all_to_all(attended_rows, 'head', split_axis=0, concat_axis=1, tiled=...  21.8 us
    all_to_all x1, blocking collectives, per_device(): lax.all_to_all(key_states, 'head', split_axis=1, concat_axis=0, tiled=True)  19.8 us
    reduce_sum x8, other arithmetic, one_tile(): new_sum = running_sum * factor + jnp.sum(weights, axis=3)  16.3 us
    all_to_all x1, blocking collectives, per_device(): lax.all_to_all(value_states, 'head', split_axis=1, concat_axis=0, tiled=T...  12.2 us
  transfers between devices with their start and end apart: 3, of which 3 were waited for; matrix products, arithmetic and copies ran while one was open for 2% of the time, Pallas kernels for 0%

commit v1 on v0

v1 whole, which is shorter than its diff:
```python
import functools
import math

import jax
import jax.numpy as jnp
from jax import lax
from jax.experimental import pallas as pl
from jax.experimental.pallas import tpu as pltpu
from jax.sharding import PartitionSpec as P

MESH = pl.DeviceIdType.MESH
HD = 128
CHUNK = 32
GROUP = 8
CTX = 8192
SUMMARY_AT = 7168
KEYS = 512
NEG = -1e30
RATE = math.log2(math.e) / math.sqrt(HD)


class Place:
    def __init__(self):
        s, h = lax.axis_index("seq"), lax.axis_index("head")
        self.x, self.zb, self.p, self.core = s // 8, s // 4 % 2, s // 2 % 2, s % 2
        self.y, self.zhi = h // 2, h % 2
        self.group = self.y * 2 + self.p
        self.zp = self.zhi * 2 + self.zb
        self.late = jnp.logical_and(self.x == 3, self.zb == 1)

    def device(self, x=None, y=None, zp=None, p=None, core=None):
        x = self.x if x is None else x
        y = self.y if y is None else y
        zp = self.zp if zp is None else zp
        p = self.p if p is None else p
        core = self.core if core is None else core
        return ((x * 4 + (zp % 2) * 2 + p) * 2 + core, y * 2 + zp // 2)

    def partner(self, group):
        return self.device(y=group // 2, p=group % 2)

    def summary_worker(self, group):
        return self.device(x=self.y, y=group // 2, zp=self.zhi * 2 + self.p, p=group % 2)

    def summary_owner(self):
        return self.device(x=3, y=self.x, zp=self.zhi * 2 + 1, p=self.zb)

    def own_summary(self):
        return jnp.logical_and(self.late, jnp.logical_and(self.y == 3, self.p == 1))


def xor_bits(value, i):
    out = 0
    for b in (4, 2, 1):
        bit = value // b % 2
        out = out + b * ((1 - bit) if i & b else bit)
    return out


def slot_of(group):
    return group % 2 * 4 + group // 2


def cols(group, width):
    return pl.ds(pl.multiple_of(group * width, width), width)


def spread_kernel(q_ref, k_ref, v_ref, qg_ref, kv_ref, qs, qr, ks, kr, zxs, zxr, ls):
    me = Place()
    barrier = pltpu.get_barrier_semaphore()

    def greet(device):
        pl.semaphore_signal(barrier, inc=1, device_id=device, device_id_type=MESH)

    ring = {
        "z+": me.device(zp=(me.zp + 1) % 4),
        "z-": me.device(zp=(me.zp + 3) % 4),
        "x+": me.device(x=(me.x + 1) % 4),
        "x-": me.device(x=(me.x + 3) % 4),
        "t": me.device(core=1 - me.core),
    }
    own_sum = me.own_summary()
    for i in range(1, 8):
        greet(me.partner(xor_bits(me.group, i)))
    for device in ring.values():
        greet(device)

    @pl.when(jnp.logical_not(own_sum))
    def _():
        greet(me.summary_owner())

    readers = jnp.where(me.late, jnp.where(own_sum, 7, 8), 0)
    pl.semaphore_wait(barrier, 12 + readers)

    def copy(src, dst, send, recv, device):
        return pltpu.make_async_remote_copy(
            src_ref=src, dst_ref=dst, send_sem=send, recv_sem=recv, device_id=device, device_id_type=MESH
        )

    def kv_at(t, group):
        return kv_ref.at[t, me.x * 2 + me.zb, group % 2, me.core, group // 2, me.zhi]

    first = []
    for i in range(8):
        group = xor_bits(me.group, i)
        for t, ref in enumerate((k_ref, v_ref)):
            src = ref.at[:, cols(group, HD)]
            if i == 0:
                c = pltpu.make_async_copy(src, kv_at(t, me.group), ls.at[t])
            else:
                c = copy(src, kv_at(t, me.group), ks.at[i, t], kr.at[i, t], me.partner(group))
            c.start()
            first.append((i, t, c))

    def q_copy(i, summary):
        group = xor_bits(me.group, i)
        src = q_ref.at[:, cols(group, GROUP * HD)]
        if summary:
            return src, copy(src, qg_ref.at[8], qs.at[i], qr.at[8], me.summary_worker(group))
        return src, copy(src, qg_ref.at[slot_of(me.group)], qs.at[i], qr.at[i], me.partner(group))

    own_q = q_ref.at[:, cols(me.group, GROUP * HD)]
    local_q = pltpu.make_async_copy(own_q, qg_ref.at[slot_of(me.group)], ls.at[2])

    @pl.when(jnp.logical_not(me.late))
    def _():
        local_q.start()
        for i in range(1, 8):
            q_copy(i, False)[1].start()

    @pl.when(me.late)
    def _():
        for i in range(8):
            src, c = q_copy(i, True)
            if i == 0:

                @pl.when(own_sum)
                def _():
                    pltpu.make_async_copy(src, qg_ref.at[8], ls.at[2]).start()

                @pl.when(jnp.logical_not(own_sum))
                def _():
                    c.start()
            else:
                c.start()

    for i, t, c in first:
        if i == 0:
            c.wait()
        else:
            group = xor_bits(me.group, i)
            src = k_ref.at[:, cols(group, HD)]
            copy(src, kv_at(t, group), ks.at[i, t], kr.at[i, t], me.partner(group)).wait_recv()

    keys = {}

    def number(kind, dx, dz, t):
        return keys.setdefault((kind, dx, dz, t), len(keys))

    def piece(dx, dz, t):
        x, zp = (me.x + dx) % 4, (me.zp + dz) % 4
        return kv_ref.at[t, x * 2 + zp % 2, :, me.core, :, zp // 2]

    def far_piece(dx, dz, t):
        x, zp = (me.x + dx) % 4, (me.zp + dz) % 4
        return kv_ref.at[t, x * 2 + zp % 2, :, 1 - me.core, :, zp // 2]

    shift = {"z+": (0, -1), "z-": (0, 1), "x+": (-1, 0), "x-": (1, 0), "t": (0, 0)}
    sent = []

    def send(dx, dz, t, *ways):
        for way in ways:
            rx, rz = (dx + shift[way][0]) % 4, (dz + shift[way][1]) % 4
            n = number(way[0], rx, rz, t)
            ref = piece(dx, dz, t)
            c = copy(ref, ref, zxs.at[n], zxr.at[n], ring[way])
            c.start()
            sent.append(c)

    def wait(kind, dx, dz, t):
        n = number(kind, dx, dz, t)
        ref = far_piece(dx, dz, t) if kind == "t" else piece(dx, dz, t)
        copy(ref, ref, zxs.at[n], zxr.at[n], ring["t"]).wait_recv()

    for t in (0, 1):
        send(0, 0, t, "z+", "z-")
    for t in (0, 1):
        send(0, 0, t, "x+", "x-", "t")
    for dz, t in ((3, 0), (1, 1)):
        wait("z", 0, dz, t)
        send(0, dz, t, "z-" if t else "z+", "x+", "x-", "t")
    for dz, t in ((3, 1), (1, 0)):
        wait("z", 0, dz, t)
        send(0, dz, t, "x+", "x-", "t")
    for dx, t in ((3, 0), (1, 1)):
        wait("x", dx, 0, t)
        send(dx, 0, t, "x-" if t else "x+", "t")
    for dz, t in ((2, 0), (2, 1)):
        wait("z", 0, dz, t)
        send(0, dz, t, "x+", "x-", "t")
    for dx, t in ((3, 1), (1, 0)):
        wait("x", dx, 0, t)
        send(dx, 0, t, "t")
    for dz in (3, 1, 2):
        for dx, t in ((3, 0), (1, 1)):
            wait("x", dx, dz, t)
            send(dx, dz, t, "x-" if t else "x+", "t")
        for dx, t in ((3, 1), (1, 0)):
            wait("x", dx, dz, t)
            send(dx, dz, t, "t")
    for dz in (0, 3, 1, 2):
        for t in (0, 1):
            wait("x", 2, dz, t)
            send(2, dz, t, "t")
    for dx in range(4):
        for dz in range(4):
            for t in (0, 1):
                wait("t", dx, dz, t)

    for c in sent:
        c.wait_send()
    for i, t, c in first:
        if i:
            c.wait_send()

    @pl.when(jnp.logical_not(me.late))
    def _():
        local_q.wait()
        for i in range(1, 8):
            q_copy(i, False)[1].wait_send()
        for i in range(1, 8):
            group = xor_bits(me.group, i)
            src = q_ref.at[:, cols(group, GROUP * HD)]
            copy(src, qg_ref.at[slot_of(group)], qs.at[i], qr.at[i], me.partner(group)).wait_recv()

    @pl.when(me.late)
    def _():
        for i in range(8):
            src, c = q_copy(i, True)
            if i == 0:

                @pl.when(own_sum)
                def _():
                    pltpu.make_async_copy(src, qg_ref.at[8], ls.at[2]).wait()

                @pl.when(jnp.logical_not(own_sum))
                def _():
                    c.wait_send()
            else:
                c.wait_send()

    @pl.when(jnp.logical_not(own_sum))
    def _():
        src = q_ref.at[:, cols(me.group, GROUP * HD)]
        copy(src, qg_ref.at[8], qs.at[0], qr.at[8], me.summary_owner()).wait_recv()


def collect_kernel(og_ref, out_ref, ss, rs, ls):
    me = Place()
    barrier = pltpu.get_barrier_semaphore()

    def greet(device):
        pl.semaphore_signal(barrier, inc=1, device_id=device, device_id_type=MESH)

    own_sum = me.own_summary()
    early = jnp.logical_not(me.late)

    @pl.when(early)
    def _():
        for i in range(1, 8):
            greet(me.partner(xor_bits(me.group, i)))

    @pl.when(me.late)
    def _():
        for i in range(1, 8):
            greet(me.summary_worker(xor_bits(me.group, i)))

        @pl.when(jnp.logical_not(own_sum))
        def _():
            greet(me.summary_worker(me.group))

    @pl.when(jnp.logical_not(own_sum))
    def _():
        pl.semaphore_wait(barrier, jnp.where(early, 8, 1))

    def copy(src, dst, send, recv, device):
        return pltpu.make_async_remote_copy(
            src_ref=src, dst_ref=dst, send_sem=send, recv_sem=recv, device_id=device, device_id_type=MESH
        )

    mine = out_ref.at[:, cols(me.group, GROUP * HD)]

    def own_copy(i):
        group = xor_bits(me.group, i)
        return copy(og_ref.at[slot_of(group)], mine, ss.at[i], rs.at[i], me.partner(group))

    summary_copy = copy(og_ref.at[8], mine, ss.at[8], rs.at[8 + me.group], me.summary_owner())
    local = pltpu.make_async_copy(og_ref.at[slot_of(me.group)], mine, ls.at[0])
    local_summary = pltpu.make_async_copy(og_ref.at[8], mine, ls.at[1])

    @pl.when(own_sum)
    def _():
        local_summary.start()

    @pl.when(jnp.logical_not(own_sum))
    def _():
        summary_copy.start()

    @pl.when(early)
    def _():
        for i in range(1, 8):
            own_copy(i).start()
        local.start()
        local.wait()
        for i in range(1, 8):
            group = xor_bits(me.group, i)
            dst = out_ref.at[:, cols(group, GROUP * HD)]
            copy(og_ref.at[slot_of(group)], dst, ss.at[i], rs.at[i], me.partner(group)).wait_recv()
        for i in range(1, 8):
            own_copy(i).wait_send()

    @pl.when(own_sum)
    def _():
        local_summary.wait()

    @pl.when(jnp.logical_not(own_sum))
    def _():
        summary_copy.wait_send()

    @pl.when(me.late)
    def _():
        for group in range(8):
            dst = out_ref.at[:, pl.ds(group * GROUP * HD, GROUP * HD)]
            c = copy(og_ref.at[8], dst, ss.at[8], rs.at[8 + group], me.partner(group))

            @pl.when(jnp.logical_not(jnp.logical_and(own_sum, me.group == group)))
            def _():
                c.wait_recv()


def attend_kernel(starts, q_hbm, kv_hbm, o_ref, qv, kv, qh, top, tot, acc, sems):
    me = Place()
    cq = pltpu.make_async_copy(q_hbm, qv, sems.at[0])
    cq.start()
    span = 1024
    loads = []
    for b in range(CTX // span):
        part = pl.ds(b * span, span)
        c = pltpu.make_async_copy(kv_hbm.at[:, part], kv.at[:, part], sems.at[1 + b])
        c.start()
        loads.append(c)
    cq.wait()
    rows = 4 * CHUNK
    for cl in range(2):
        for h in range(GROUP):
            for y in range(4):
                at = cl * GROUP * rows + h * rows + y * CHUNK
                qh[at : at + CHUNK] = qv[cl * 4 + y, :, h * HD : (h + 1) * HD]
    base = 2 * GROUP * rows
    for h in range(GROUP):
        qh[base + h * CHUNK : base + (h + 1) * CHUNK] = qv[8, :, h * HD : (h + 1) * HD]
    top[...] = jnp.full_like(top, NEG)
    tot[...] = jnp.zeros_like(tot)
    acc[...] = jnp.zeros_like(acc)
    for c in loads:
        c.wait()

    def tile(at, m, key_at, visible):
        part = pl.ds(at, m)
        keys = pl.ds(pl.multiple_of(key_at, HD), KEYS)
        s = lax.dot_general(
            qh[part], kv[0, keys], (((1,), (1,)), ((), ())), preferred_element_type=jnp.float32
        )
        if visible is not None:
            s = jnp.where(visible, s, NEG)
        old = top[part]
        new = jnp.maximum(old, jnp.max(s, axis=1, keepdims=True))
        top[part] = new
        w = jnp.exp2(s * RATE - jnp.concatenate([new * RATE] * (KEYS // 128), axis=1))
        factor = jnp.exp2((old - new) * RATE)
        lanes = w[:, :128]
        for j in range(1, KEYS // 128):
            lanes = lanes + w[:, j * 128 : (j + 1) * 128]
        tot[part] = tot[part] * factor + lanes
        acc[part] = acc[part] * factor + jnp.dot(
            w.astype(jnp.bfloat16), kv[1, keys], preferred_element_type=jnp.float32
        )

    def key_pos(m, key_at):
        return key_at + lax.broadcasted_iota(jnp.int32, (m, KEYS), 1)

    m = GROUP * CHUNK
    chunk = (me.zb * 2 + me.core) * 8 + me.x * 2 + me.zhi
    sum_pos = SUMMARY_AT + chunk * CHUNK + lax.broadcasted_iota(jnp.int32, (m, KEYS), 0) % CHUNK

    def summary_step(b, _):
        tile(base, m, b * KEYS, None)
        return 0

    lax.fori_loop(0, SUMMARY_AT // KEYS, summary_step, 0)
    for b in range(SUMMARY_AT // KEYS, CTX // KEYS):
        tile(base, m, b * KEYS, key_pos(m, b * KEYS) <= sum_pos)

    first_response = starts[1]

    @pl.when(jnp.logical_not(me.late))
    def _():
        for cl in range(2):
            p0 = (((me.x * 2 + me.zb) * 2 + cl) * 2 + me.core) * 256
            r = lax.broadcasted_iota(jnp.int32, (rows, 1), 0)
            pos = p0 + r // CHUNK * 64 + me.zhi * CHUNK + r % CHUNK
            own = jnp.zeros_like(pos)
            own_low = jnp.int32(0)
            own_high = jnp.int32(0)
            for j in range(10):
                own = jnp.where(starts[j] <= pos, starts[j], own)
                own_low = jnp.where(starts[j] <= p0, starts[j], own_low)
                own_high = jnp.where(starts[j] <= p0 + 255, starts[j], own_high)
            end = jnp.minimum(first_response, pos + 1)
            begin = jnp.maximum(first_response, own)
            here = cl * GROUP * rows

            def step(key_at, visible):
                for h in range(0, GROUP, 2):
                    both = None if visible is None else jnp.concatenate([visible, visible], axis=0)
                    tile(here + h * rows, 2 * rows, key_at, both)

            def prompt_step(b, _):
                key_at = b * KEYS
                clear = key_at + KEYS <= jnp.minimum(first_response, p0 + 1)

                @pl.when(clear)
                def _():
                    step(key_at, None)

                @pl.when(jnp.logical_not(clear))
                def _():
                    step(key_at, key_pos(rows, key_at) < end)

                return 0

            lax.fori_loop(0, (jnp.minimum(first_response, p0 + 256) + KEYS - 1) // KEYS, prompt_step, 0)
            low = jnp.maximum(own_low, first_response) // HD * HD
            high = jnp.maximum(own_high, first_response)

            def own_step(b, _):
                key_at = low + b * KEYS
                clear = jnp.logical_and(key_at >= high, key_at + KEYS <= p0 + 1)

                @pl.when(clear)
                def _():
                    step(key_at, None)

                @pl.when(jnp.logical_not(clear))
                def _():
                    k = key_pos(rows, key_at)
                    step(key_at, jnp.logical_and(k >= begin, k <= pos))

                return 0

            lax.fori_loop(0, (jnp.maximum(p0 + 256 - low, 0) + KEYS - 1) // KEYS, own_step, 0)

    def finish(at, m):
        part = pl.ds(at, m)
        return (acc[part] / jnp.sum(tot[part], axis=1, keepdims=True)).astype(o_ref.dtype)

    @pl.when(jnp.logical_not(me.late))
    def _():
        for cl in range(2):
            for h in range(GROUP):
                done = finish(cl * GROUP * rows + h * rows, rows)
                for y in range(4):
                    o_ref[cl * 4 + y, :, h * HD : (h + 1) * HD] = done[y * CHUNK : (y + 1) * CHUNK]

    for h in range(GROUP):
        o_ref[8, :, h * HD : (h + 1) * HD] = finish(base + h * CHUNK, CHUNK)


def per_device(query_states, key_states, value_states, seg_ids, seg_starts):
    anywhere = pl.BlockSpec(memory_space=pl.ANY)
    dma = pltpu.SemaphoreType.DMA
    qg, kv = pl.pallas_call(
        spread_kernel,
        out_shape=(
            jax.ShapeDtypeStruct((9, CHUNK, GROUP * HD), jnp.bfloat16),
            jax.ShapeDtypeStruct((2, 8, 2, 2, 4, 2, CHUNK, HD), jnp.bfloat16),
        ),
        in_specs=[anywhere] * 3,
        out_specs=(anywhere, anywhere),
        scratch_shapes=[dma((8,)), dma((9,)), dma((8, 2)), dma((8, 2)), dma((62,)), dma((62,)), dma((3,))],
        compiler_params=pltpu.CompilerParams(collective_id=0, has_side_effects=True),
        name="spread",
    )(query_states, key_states, value_states)
    lanes = 2 * GROUP * 4 * CHUNK + GROUP * CHUNK
    og = pl.pallas_call(
        attend_kernel,
        out_shape=jax.ShapeDtypeStruct((9, CHUNK, GROUP * HD), jnp.bfloat16),
        in_specs=[pl.BlockSpec(memory_space=pltpu.SMEM), anywhere, anywhere],
        out_specs=pl.BlockSpec(memory_space=pltpu.VMEM),
        scratch_shapes=[
            pltpu.VMEM((9, CHUNK, GROUP * HD), jnp.bfloat16),
            pltpu.VMEM((2, CTX, HD), jnp.bfloat16),
            pltpu.VMEM((lanes, HD), jnp.bfloat16),
            pltpu.VMEM((lanes, 128), jnp.float32),
            pltpu.VMEM((lanes, 128), jnp.float32),
            pltpu.VMEM((lanes, HD), jnp.float32),
            dma((9,)),
        ],
        compiler_params=pltpu.CompilerParams(vmem_limit_bytes=48 * 1024 * 1024),
        name="attend",
    )(seg_starts, qg, kv.reshape(2, CTX, HD))
    return pl.pallas_call(
        collect_kernel,
        out_shape=jax.ShapeDtypeStruct((CHUNK, 8 * GROUP * HD), jnp.bfloat16),
        in_specs=[anywhere],
        out_specs=anywhere,
        scratch_shapes=[dma((9,)), dma((16,)), dma((2,))],
        compiler_params=pltpu.CompilerParams(collective_id=1, has_side_effects=True),
        name="collect",
    )(og)


def solution(mesh):
    return jax.shard_map(
        per_device,
        mesh=mesh,
        in_specs=(
            P(("seq", "head"), None),
            P(("seq", "head"), None),
            P(("seq", "head"), None),
            P("seq"),
            P(),
        ),
        out_specs=P(("seq", "head"), None),
        check_vma=False,
    )
```

time: 320 us -> 85.3 us (0.27)
  the two profiles are of different devices: /device:TPU:3 before, /device:TPU:2 now
where the time goes in v1:
time: 85.3 us; the launch traced here: 85.1 us
  Pallas kernels  78.4 us (92%)
  local copies, waits for them, and re-layouts  6.59 us (8%)
    pallas_call x1, Pallas kernels, per_device(): pl.pallas_call(spread_kernel, out_shape=(jax.ShapeDtypeStruct((9, CHUNK,...  44.2 us
    pallas_call x1, Pallas kernels, per_device(): pl.pallas_call(attend_kernel, out_shape=jax.ShapeDtypeStruct((9, CHUNK, G...  23.1 us
    pallas_call x1, Pallas kernels, per_device(): pl.pallas_call(collect_kernel, out_shape=jax.ShapeDtypeStruct((CHUNK, 8 *...  11.1 us
    unnamed x9, local copies, waits for them, and re-layouts  6.59 us

profile of v1, /device:TPU:2, one launch (start us, length us, event | category | flops | bytes accessed | tf_op | source)
XLA Modules:
  0.0 85.1 jit_solution(15486866930301626122)
XLA Ops:
  0.0 44.2 %spread.1 = (bf16[9,32,1024]{2,1,0:T(8,128)(2,1)}, bf16[2,8,2,2,4,2,32,128]{7,6,5,4,3,2,1,0:T(8,128)(2,1)}) custom-call(bf16[32,8192]{1,0:T(8,128)(2,1)} %q_ref.1, bf16[32,1024]{1,0:T(8,128)(2,1)} %k_ref.1, bf16[32,1024]{1,0:T(8,128)(2,1)} %v_ref.1), custom_call_target="tpu_custom_call" | custom-call | tf_op jit(solution)/shard_map/spread/pallas_call | solution.py:482
  44.2 0.0 copy-start
  44.3 2.2 %copy-done = bf16[2,8,2,2,4,2,32,128]{7,6,5,4,3,2,1,0:T(8,128)(2,1)S(1)} copy-done((bf16[2,8,2,2,4,2,32,128]{7,6,5,4,3,2,1,0:T(8,128)(2,1)S(1)}, bf16[2,8,2,2,4,2,32,128]{7,6,5,4,3,2,1,0:T(8,128)(2,1)}, u32[]{:S(2)}) %copy-start) | copy-done | bytes 4194328
  46.4 0.0 copy-start.2
  46.4 1.1 %copy-done.2 = bf16[9,32,1024]{2,1,0:T(8,128)(2,1)S(1)} copy-done((bf16[9,32,1024]{2,1,0:T(8,128)(2,1)S(1)}, bf16[9,32,1024]{2,1,0:T(8,128)(2,1)}, u32[]{:S(2)}) %copy-start.2) | copy-done | bytes 589848
  47.5 0.0 copy-start.3
  47.5 0.7 copy-done.3
  48.2 23.1 %attend.1.og_ref = bf16[9,32,1024]{2,1,0:T(8,128)(2,1)S(1)} custom-call(s32[10]{0:T(128)S(1)} %copy-done.3, bf16[9,32,1024]{2,1,0:T(8,128)(2,1)S(1)} %copy-done.2, bf16[2,8192,128]{2,1,0:T(8,128)(2,1)S(1)} %bitcast.1), custom_call_target="tpu_custom_call" | custom-call | tf_op jit(solution)/shard_map/attend/pallas_call | solution.py:495
  71.2 0.0 copy-start.1
  71.2 0.8 copy-done.1
  72.1 11.1 %collect.1 = bf16[32,8192]{1,0:T(8,128)(2,1)} custom-call(bf16[9,32,1024]{2,1,0:T(8,128)(2,1)} %copy-done.1), custom_call_target="tpu_custom_call" | custom-call | tf_op jit(solution)/shard_map/collect/pallas_call | solution.py:512
  83.2 1.9 %copy.6 = bf16[32,8192]{1,0:T(8,128)(2,1)} copy(bf16[32,8192]{1,0:T(8,128)(2,1)} %collect.1) | data formatting | bytes 1048576
Async XLA Ops:
  44.2 2.2 %copy-start = (bf16[2,8,2,2,4,2,32,128]{7,6,5,4,3,2,1,0:T(8,128)(2,1)S(1)}, bf16[2,8,2,2,4,2,32,128]{7,6,5,4,3,2,1,0:T(8,128)(2,1)}, u32[]{:S(2)}) copy-start(bf16[2,8,2,2,4,2,32,128]{7,6,5,4,3,2,1,0:T(8,128)(2,1)} %get-tuple-element.8) | copy-start | bytes 12582916
  46.4 1.1 %copy-start.2 = (bf16[9,32,1024]{2,1,0:T(8,128)(2,1)S(1)}, bf16[9,32,1024]{2,1,0:T(8,128)(2,1)}, u32[]{:S(2)}) copy-start(bf16[9,32,1024]{2,1,0:T(8,128)(2,1)} %get-tuple-element.7.q_hbm) | copy-start | bytes 1769476
  47.5 0.7 copy-start.3
  71.2 0.8 copy-start.1
